TPU v7x, 256 devices: a whole 4x4x8 slice. The times are simulated.
256 devices in a mesh: island: 8 (over y_hi, x), fsdp: 32 (over y_lo, z, core).
Axes of the slice: x: 4, y: 4 (y_hi: 2, y_lo: 2; y = y_hi * 2 + y_lo), z: 8, core: 2. Of those that a mesh axis runs over, the one named last changes fastest.
Arguments:
- hidden_in: bfloat16 [8, 8192, 8192], P('island', 'fsdp'), may hold values from -6 to 6
- norm_gain: bfloat16 [8, 8192], P('island'), may hold values from 0.5 to 2
- key_weight: bfloat16 [8, 8192, 512], P('island', 'fsdp'), may hold values from -0.0625 to 0.0625
- key_cotangent: bfloat16 [8, 8192, 512], P('island', 'fsdp'), may hold values from -6 to 6
- frag_global: float32 [8192, 512], P('fsdp'), may hold values from -6 to 6
- frag_moment: float32 [8192, 512], P('fsdp'), may hold values from -4 to 4
- frag_local: bfloat16 [8, 8192, 512], P('island', 'fsdp'), may hold values from -6 to 6
Outputs:
- keys: bfloat16 [8, 8192, 512], P('island', 'fsdp')
- grad_in: bfloat16 [8, 8192, 8192], P('island', 'fsdp')
- grad_w: float32 [8, 8192, 512], P('island', 'fsdp')
- new_global: float32 [8192, 512], P('fsdp')
- new_moment: float32 [8192, 512], P('fsdp')
- new_local: bfloat16 [8, 8192, 512], P('island', 'fsdp')
All inputs are finite; a program needn't handle non-finite values.
Results may differ from a plain program's by a relative error of at most 0.0049.
Values may be sent and summed in bfloat16 or wider, within the bound.
A program may use at most 128 MiB of HBM per device.

v0:
```python
import jax
import jax.numpy as jnp
from jax import lax
from jax.sharding import PartitionSpec as P

epsilon = 1e-05
outer_rate = 0.7
outer_momentum = 0.9
mix_weight = 0.5


def nesterov(pseudo, moment, params):
    new_moment = outer_momentum * moment + pseudo
    new_params = params - outer_rate * (pseudo + outer_momentum * new_moment)
    return (new_moment, new_params)


def body(hidden_in, norm_gain, key_weight, key_cotangent, frag_global, frag_moment, frag_local):
    hidden_f = hidden_in[0].astype(jnp.float32)
    gain_f = norm_gain[0].astype(jnp.float32)
    scale = lax.rsqrt(jnp.mean(hidden_f * hidden_f, axis=-1, keepdims=True) + epsilon)
    normed = (hidden_f * scale * gain_f).astype(jnp.bfloat16)
    cotangent = key_cotangent[0]
    gathered = lax.all_gather(key_weight, "fsdp", axis=1, tiled=True)[0]
    key_sum = jnp.dot(normed, gathered, preferred_element_type=jnp.float32)
    back = jnp.einsum("tk,dk->td", cotangent, gathered, preferred_element_type=jnp.float32)
    keys = key_sum.astype(jnp.bfloat16)
    upper = back * gain_f
    inner = jnp.mean(upper * hidden_f, axis=-1, keepdims=True)
    grad_in = (scale * upper - hidden_f * scale * scale * scale * inner).astype(jnp.bfloat16)
    grad_w = lax.psum_scatter(
        jnp.einsum("td,tk->dk", normed, cotangent, preferred_element_type=jnp.float32),
        "fsdp",
        scatter_dimension=0,
        tiled=True,
    )
    islands = lax.axis_size("island")
    local_f = frag_local[0].astype(jnp.float32)
    difference = frag_global - local_f
    summed = lax.psum(difference, "island")
    new_moment, new_global = nesterov(summed / islands, frag_moment, frag_global)
    new_local = (mix_weight * local_f + (1.0 - mix_weight) * new_global).astype(jnp.bfloat16)
    return (keys[None], grad_in[None], grad_w[None], new_global, new_moment, new_local[None])


def solution(mesh):
    in_specs = (
        P("island", "fsdp", None),
        P("island", None),
        P("island", "fsdp", None),
        P("island", "fsdp", None),
        P("fsdp", None),
        P("fsdp", None),
        P("island", "fsdp", None),
    )
    out_specs = (
        P("island", "fsdp", None),
        P("island", "fsdp", None),
        P("island", "fsdp", None),
        P("fsdp", None),
        P("fsdp", None),
        P("island", "fsdp", None),
    )
    return jax.shard_map(body, mesh=mesh, in_specs=in_specs, out_specs=out_specs, check_vma=False)
```

profile of v0, /device:TPU:2, one launch (start us, length us, event | category | flops | bytes accessed | tf_op | source)
XLA Modules:
  0.0 257.9 jit_solution(416443387016718516)
XLA Ops:
  8.0 0.0 copy-start
  8.0 0.0 all-gather.2.cloned.1.call-start
  8.1 0.7 all-gather.2.cloned.1.call-update
  8.7 0.0 all-reduce.2.cloned.1.call-start
  8.8 2.0 convert_subtract_fusion
  10.8 0.0 all-reduce.2.cloned.1.call-update
  10.8 0.0 reduce-scatter.2.cloned.1.call-start
  10.8 0.8 mul.110
  11.6 74.3 %all-gather.2.cloned.1.call-done = bf16[1,8192,512]{2,1,0:T(8,128)(2,1)} async-done(((bf16[1,256,512]{2,1,0:T(8,128)(2,1)}), bf16[1,8192,512]{2,1,0:T(8,128)(2,1)}) %all-gather.2.cloned.1.call-update) | async-done | bytes 8388624 | tf_op jit(solution)/shard_map/all_gather | solution.py:24
  86.0 0.0 copy-done
  86.0 0.0 copy-start.1
  86.0 11.9 %fusion.9 = (f32[256]{0:T(256)S(1)}, f32[256]{0:T(256)S(1)}, f32[256,8192]{1,0:T(8,128)}) fusion(bf16[1,256,8192]{2,1,0:T(8,128)(2,1)} %param.7, f32[8192]{0:T(1024)S(1)} %bitcast.62, bf16[1,8192,512]{2,1,0:T(8,128)(2,1)} %all-gather.2.cloned.1.call-done, bf16[1,256,512]{2,1,0:T(8,128)(2,1)S(1)} %copy-done), kind=kOutput, calls=%fused_computation.12 | convolution fusion | flops 2160066048 | bytes 21268480 | tf_op jit(solution)/shard_map/tk,dk->td/dot_general | solution.py:26
  97.9 0.0 copy-done.1
  97.9 8.3 %fusion.20 = f32[8192,512]{1,0:T(8,128)} fusion(bf16[1,256,8192]{2,1,0:T(8,128)(2,1)S(1)} %copy-done.1, f32[8192]{0:T(1024)S(1)} %bitcast.63, f32[256]{0:T(256)S(1)} %add_rsqrt_fusion, bf16[1,256,512]{2,1,0:T(8,128)(2,1)S(1)} %copy-done), kind=kOutput, calls=%fused_computation.21 | convolution fusion | flops 2155872256 | bytes 21267456 | tf_op jit(solution)/shard_map/td,tk->dk/dot_general | solution.py:32
  106.2 0.0 copy-start.3
  106.2 0.0 copy-start.4
  106.2 0.0 copy-start.5
  106.2 0.0 reduce-scatter.2.cloned.1.call-update
  106.2 0.0 all-reduce.2.cloned.1.call-done
  106.3 1.0 copy-done.3
  107.3 0.1 copy-done.4
  107.3 0.2 copy-done.5
  107.5 0.0 slice-start
  107.5 2.4 fusion.30
  109.9 0.0 copy-start.2
  109.9 0.0 slice-start.1
  109.9 7.9 %fusion.23 = bf16[1,256,512]{2,1,0:T(8,128)(2,1)} fusion(bf16[1,8192,512]{2,1,0:T(8,128)(2,1)} %all-gather.2.cloned.1.call-done, bf16[1,256,8192]{2,1,0:T(8,128)(2,1)} %param.7, f32[8192]{0:T(1024)S(1)} %bitcast.64, f32[256]{0:T(256)S(1)} %add_rsqrt_fusion), kind=kOutput, calls=%fused_computation.22 | convolution fusion | flops 2156003328 | bytes 12878848 | tf_op jit(solution)/shard_map/dot_general | solution.py:25
  117.8 0.0 slice-done
  117.8 0.0 copy-done.2
  117.8 0.0 slice-done.1
  117.8 3.7 %fusion.16 = bf16[1,256,8192]{2,1,0:T(8,128)(2,1)} fusion(bf16[1,256,8192]{2,1,0:T(8,128)(2,1)S(1)} %copy-done.2, f32[256,8192]{1,0:T(8,128)S(1)} %bitcast.61, f32[256]{0:T(256)S(1)} %broadcast_multiply_fusion, f32[256]{0:T(256)S(1)} %add_rsqrt_fusion), kind=kLoop, calls=%fused_computation.19 | loop fusion | flops 16777216 | bytes 16779264 | tf_op jit(solution)/shard_map/broadcast_in_dim | solution.py:43
  121.6 128.9 %reduce-scatter.2.cloned.1.call-done = f32[256,512]{1,0:T(8,128)} async-done(((f32[8192,512]{1,0:T(8,128)}), f32[256,512]{1,0:T(8,128)}) %reduce-scatter.2.cloned.1.call-update) | async-done | bytes 524304 | tf_op jit(solution)/shard_map/reduce_scatter | solution.py:31
  (3 shorter events, 0.0 us)
Async XLA Ops:
  8.0 78.0 %copy-start = (bf16[1,256,512]{2,1,0:T(8,128)(2,1)S(1)}, bf16[1,256,512]{2,1,0:T(8,128)(2,1)}, u32[]{:S(2)}) copy-start(bf16[1,256,512]{2,1,0:T(8,128)(2,1)} %param.10) | copy-start | bytes 786436
  8.0 78.0 %all-gather.2.cloned.1.call-start = ((), (), s32[]{:S(2)}) async-start(), calls=%async_computation.1 | async-start | bytes 8650752 | tf_op jit(solution)/shard_map/all_gather | solution.py:24
  8.7 97.5 %all-reduce.2.cloned.1.call-start = ((), (), s32[]{:S(2)}) async-start(), calls=%async_computation.3 | async-start | bytes 1048576 | tf_op jit(solution)/shard_map/psum | solution.py:40
  10.8 239.6 %reduce-scatter.2.cloned.1.call-start = ((), (), s32[]{:S(2)}) async-start(), calls=%async_computation.2 | async-start | bytes 17301504 | tf_op jit(solution)/shard_map/reduce_scatter | solution.py:31
  86.0 12.0 %copy-start.1 = (bf16[1,256,8192]{2,1,0:T(8,128)(2,1)S(1)}, bf16[1,256,8192]{2,1,0:T(8,128)(2,1)}, u32[]{:S(2)}) copy-start(bf16[1,256,8192]{2,1,0:T(8,128)(2,1)} %param.7) | copy-start | bytes 12582916
  106.2 1.0 copy-start.3
  106.2 1.1 copy-start.4
  106.2 1.3 copy-start.5
  107.5 10.3 %slice-start = ((s8[8388608]{0:T(1024)(128)(4,1)}), s8[4194304]{0:T(1024)(128)(4,1)S(1)}, s32[]{:S(2)}) async-start(s8[8388608]{0:T(1024)(128)(4,1)} %bitcast.60), calls=%async_computation.4 | async-start | bytes 8388608
  109.9 7.9 %copy-start.2 = (bf16[1,256,8192]{2,1,0:T(8,128)(2,1)S(1)}, bf16[1,256,8192]{2,1,0:T(8,128)(2,1)}, u32[]{:S(2)}) copy-start(bf16[1,256,8192]{2,1,0:T(8,128)(2,1)} %param.7) | copy-start | bytes 12582916
  109.9 7.9 %slice-start.1 = ((s8[8388608]{0:T(1024)(128)(4,1)}), s8[4194304]{0:T(1024)(128)(4,1)S(1)}, s32[]{:S(2)}) async-start(s8[8388608]{0:T(1024)(128)(4,1)} %bitcast.60), calls=%async_computation.5 | async-start | bytes 8388608
Sparse Core Ops, SparseCore 0:
  10.7 75.2 all-gather.1
  106.4 144.0 reduce-scatter.1
Sparse Core Ops, SparseCore 1:
  12.4 89.9 all-reduce.1
where the time goes:
time: 258 us
  waiting for transfers between devices  204 us (79%)
  matrix products  28.1 us (11%)
  between operations  15.5 us (6%)
  other arithmetic  8.93 us (3%)
    reduce_scatter x1, waiting for transfers between devices, body(): lax.psum_scatter(jnp.einsum('td,tk->dk', normed, cotangent, preferred_ele...  129 us
    all_gather x1, waiting for transfers between devices, body(): gathered = lax.all_gather(key_weight, 'fsdp', axis=1, tiled=True)[0]  74.3 us
    dot_general x1, matrix products, body(): jnp.einsum('tk,dk->td', cotangent, gathered, preferred_element_type=jnp.f...  11.9 us
    dot_general x1, matrix products, body(): jnp.einsum('td,tk->dk', normed, cotangent, preferred_element_type=jnp.flo...  8.27 us
    dot_general x1, matrix products, body(): key_sum = jnp.dot(normed, gathered, preferred_element_type=jnp.float32)  7.88 us
  transfers between devices with their start and end apart: 3, of which 2 were waited for; matrix products, arithmetic and copies ran while one was open for 14% of the time, Pallas kernels for 0%

commit v1 on v0

--- a/solution.py
+++ b/solution.py
@@ -21,7 +21,9 @@
     scale = lax.rsqrt(jnp.mean(hidden_f * hidden_f, axis=-1, keepdims=True) + epsilon)
     normed = (hidden_f * scale * gain_f).astype(jnp.bfloat16)
     cotangent = key_cotangent[0]
-    gathered = lax.all_gather(key_weight, "fsdp", axis=1, tiled=True)[0]
+    gathered = jnp.concatenate(
+        lax.all_to_all(jnp.stack([key_weight] * lax.axis_size("fsdp")), "fsdp", 0, 0), axis=1
+    )[0]
     key_sum = jnp.dot(normed, gathered, preferred_element_type=jnp.float32)
     back = jnp.einsum("tk,dk->td", cotangent, gathered, preferred_element_type=jnp.float32)
     keys = key_sum.astype(jnp.bfloat16)

time: 258 us -> 385 us (1.49)
  waiting for transfers between devices: 204 us -> 317 us
  starting transfers between devices: 0.12 us -> 10.2 us
  local copies, waits for them, and re-layouts: 1.24 us -> 6.19 us
    all_to_all x0 -> x1, waiting for transfers between devices: none -> 185 us  [body(): lax.all_to_all(jnp.stack([key_weight] * lax.axis_size('fsdp')), 'fsdp', 0...]
    all_gather x1 -> x0, waiting for transfers between devices: 74.3 us -> none  [body(): gathered = lax.all_gather(key_weight, 'fsdp', axis=1, tiled=True)[0]]
    all_to_all x0 -> x1, starting transfers between devices: none -> 10.1 us  [body(): lax.all_to_all(jnp.stack([key_weight] * lax.axis_size('fsdp')), 'fsdp', 0...]
    another operation x0 -> x1, local copies, waits for them, and re-layouts: none -> 5.17 us  [body(): jnp.stack([key_weight] * lax.axis_size('fsdp'))]
  transfers between devices with their start and end apart: 3 -> 3, of which waited for: 2 -> 2; matrix products, arithmetic and copies ran while one was open for 14% -> 9% of each run, Pallas kernels for 0% -> 0%
where the time goes in v1:
time: 385 us; the launch traced here: 384 us
  waiting for transfers between devices  317 us (82%)
  matrix products  28.1 us (7%)
  between operations  15.6 us (4%)
  starting transfers between devices  10.2 us (3%)
  other arithmetic  7.06 us (2%)
  local copies, waits for them, and re-layouts  6.19 us (2%)
    all_to_all x1, waiting for transfers between devices, body(): lax.all_to_all(jnp.stack([key_weight] * lax.axis_size('fsdp')), 'fsdp', 0...  185 us
    reduce_scatter x1, waiting for transfers between devices, body(): lax.psum_scatter(jnp.einsum('td,tk->dk', normed, cotangent, preferred_ele...  132 us
    dot_general x1, matrix products, body(): jnp.einsum('tk,dk->td', cotangent, gathered, preferred_element_type=jnp.f...  11.9 us
    all_to_all x1, starting transfers between devices, body(): lax.all_to_all(jnp.stack([key_weight] * lax.axis_size('fsdp')), 'fsdp', 0...  10.1 us
    dot_general x1, matrix products, body(): jnp.einsum('td,tk->dk', normed, cotangent, preferred_element_type=jnp.flo...  8.27 us
    dot_general x1, matrix products, body(): key_sum = jnp.dot(normed, gathered, preferred_element_type=jnp.float32)  7.88 us
  transfers between devices with their start and end apart: 3, of which 2 were waited for; matrix products, arithmetic and copies ran while one was open for 9% of the time, Pallas kernels for 0%

profile of v1, /device:TPU:2, one launch (start us, length us, event | category | flops | bytes accessed | tf_op | source)
XLA Modules:
  0.0 384.4 jit_solution(15409244983341434424)
XLA Ops:
  8.0 0.0 copy-start
  8.0 5.2 %stack.2 = bf16[32,1,256,512]{3,2,1,0:T(8,128)(2,1)} broadcast(bf16[256,512]{1,0:T(8,128)(2,1)} %bitcast.55), dimensions={2,3} | broadcast | bytes 8650752 | tf_op jit(solution)/shard_map/stack | solution.py:25
  13.2 0.0 copy-start.3
  13.2 0.0 copy-start.4
  13.2 0.0 copy-start.6
  13.2 10.1 %all-to-all-start = ((bf16[32,1,256,512]{3,2,1,0:T(8,128)(2,1)}), bf16[32,1,256,512]{3,2,1,0:T(8,128)(2,1)}, u32[]{:S(2)}, u32[]{:S(2)}) async-start(bf16[32,1,256,512]{3,2,1,0:T(8,128)(2,1)} %stack.2), calls=%async_computation | async-start | bytes 16777216 | tf_op jit(solution)/shard_map/all_to_all | solution.py:25
  23.3 0.0 all-reduce.2.cloned.1.call-start
  23.4 0.0 copy-done.3
  23.4 0.0 copy-done.4
  23.4 0.9 convert_subtract_fusion
  24.3 0.0 all-reduce.2.cloned.1.call-update
  24.3 0.0 reduce-scatter.2.cloned.1.call-start
  24.3 0.0 copy-done.6
  24.4 185.1 %all-to-all-done = bf16[32,1,256,512]{3,2,1,0:T(8,128)(2,1)} async-done(((bf16[32,1,256,512]{3,2,1,0:T(8,128)(2,1)}), bf16[32,1,256,512]{3,2,1,0:T(8,128)(2,1)}, u32[]{:S(2)}, u32[]{:S(2)}) %all-to-all-start) | async-done | bytes 8388640 | tf_op jit(solution)/shard_map/all_to_all | solution.py:25
  209.5 0.0 copy-done
  209.5 0.0 copy-start.1
  209.5 11.9 %fusion.9 = (f32[256]{0:T(256)S(1)}, f32[256]{0:T(256)S(1)}, f32[256,8192]{1,0:T(8,128)}) fusion(bf16[1,256,8192]{2,1,0:T(8,128)(2,1)} %param.7, f32[8192]{0:T(1024)S(1)} %bitcast.56, bf16[8192,512]{1,0:T(8,128)(2,1)} %bitcast.4, bf16[1,256,512]{2,1,0:T(8,128)(2,1)S(1)} %copy-done), kind=kOutput, calls=%fused_computation.12 | convolution fusion | flops 2160066048 | bytes 21268480 | tf_op jit(solution)/shard_map/tk,dk->td/dot_general | solution.py:28
  221.4 0.0 copy-done.1
  221.4 8.3 %fusion.14 = f32[8192,512]{1,0:T(8,128)} fusion(bf16[1,256,8192]{2,1,0:T(8,128)(2,1)S(1)} %copy-done.1, f32[8192]{0:T(1024)S(1)} %bitcast.57, f32[256]{0:T(256)S(1)} %add_rsqrt_fusion, bf16[1,256,512]{2,1,0:T(8,128)(2,1)S(1)} %copy-done), kind=kOutput, calls=%fused_computation.18 | convolution fusion | flops 2155872256 | bytes 21267456 | tf_op jit(solution)/shard_map/td,tk->dk/dot_general | solution.py:34
  229.7 0.0 copy-start.5
  229.7 0.0 reduce-scatter.2.cloned.1.call-update
  229.7 0.0 all-reduce.2.cloned.1.call-done
  229.7 1.0 copy-done.5
  230.7 0.0 slice-start
  230.7 2.4 fusion.22
  233.2 0.0 copy-start.2
  233.2 0.0 slice-start.1
  233.2 7.9 %fusion.17 = bf16[1,256,512]{2,1,0:T(8,128)(2,1)} fusion(bf16[8192,512]{1,0:T(8,128)(2,1)} %bitcast.4, bf16[1,256,8192]{2,1,0:T(8,128)(2,1)} %param.7, f32[8192]{0:T(1024)S(1)} %bitcast.58, f32[256]{0:T(256)S(1)} %add_rsqrt_fusion), kind=kOutput, calls=%fused_computation.19 | convolution fusion | flops 2156003328 | bytes 12878848 | tf_op jit(solution)/shard_map/dot_general | solution.py:27
  241.1 0.0 slice-done
  241.1 0.0 copy-done.2
  241.1 0.0 slice-done.1
  241.1 3.7 fusion.13
  244.8 132.2 %reduce-scatter.2.cloned.1.call-done = f32[256,512]{1,0:T(8,128)} async-done(((f32[8192,512]{1,0:T(8,128)}), f32[256,512]{1,0:T(8,128)}) %reduce-scatter.2.cloned.1.call-update) | async-done | bytes 524304 | tf_op jit(solution)/shard_map/reduce_scatter | solution.py:33
  (4 shorter events, 0.0 us)
Async XLA Ops:
  8.0 201.5 %copy-start = (bf16[1,256,512]{2,1,0:T(8,128)(2,1)S(1)}, bf16[1,256,512]{2,1,0:T(8,128)(2,1)}, u32[]{:S(2)}) copy-start(bf16[1,256,512]{2,1,0:T(8,128)(2,1)} %param.10) | copy-start | bytes 786436
  13.2 10.2 %copy-start.3 = (f32[256,512]{1,0:T(8,128)S(1)}, f32[256,512]{1,0:T(8,128)}, u32[]{:S(2)}) copy-start(f32[256,512]{1,0:T(8,128)} %param.11) | copy-start | bytes 1572868
  13.2 10.2 %copy-start.4 = (bf16[1,256,512]{2,1,0:T(8,128)(2,1)S(1)}, bf16[1,256,512]{2,1,0:T(8,128)(2,1)}, u32[]{:S(2)}) copy-start(bf16[1,256,512]{2,1,0:T(8,128)(2,1)} %param.13) | copy-start | bytes 786436
  13.2 11.2 %copy-start.6 = (bf16[1,8192]{1,0:T(2,128)(2,1)S(1)}, bf16[1,8192]{1,0:T(2,128)(2,1)}, u32[]{:S(2)}) copy-start(bf16[1,8192]{1,0:T(2,128)(2,1)} %param.8) | copy-start | bytes 49156
  13.2 196.3 %all-to-all-start = ((bf16[32,1,256,512]{3,2,1,0:T(8,128)(2,1)}), bf16[32,1,256,512]{3,2,1,0:T(8,128)(2,1)}, u32[]{:S(2)}, u32[]{:S(2)}) async-start(bf16[32,1,256,512]{3,2,1,0:T(8,128)(2,1)} %stack.2), calls=%async_computation | async-start | bytes 16777216 | tf_op jit(solution)/shard_map/all_to_all | solution.py:25
  23.3 206.4 %all-reduce.2.cloned.1.call-start = ((), (), s32[]{:S(2)}) async-start(), calls=%async_computation.3 | async-start | bytes 1048576 | tf_op jit(solution)/shard_map/psum | solution.py:42
  24.3 352.7 %reduce-scatter.2.cloned.1.call-start = ((), (), s32[]{:S(2)}) async-start(), calls=%async_computation.2 | async-start | bytes 17301504 | tf_op jit(solution)/shard_map/reduce_scatter | solution.py:33
  209.5 12.0 %copy-start.1 = (bf16[1,256,8192]{2,1,0:T(8,128)(2,1)S(1)}, bf16[1,256,8192]{2,1,0:T(8,128)(2,1)}, u32[]{:S(2)}) copy-start(bf16[1,256,8192]{2,1,0:T(8,128)(2,1)} %param.7) | copy-start | bytes 12582916
  229.7 1.0 copy-start.5
  230.7 10.3 %slice-start = ((s8[8388608]{0:T(1024)(128)(4,1)}), s8[4194304]{0:T(1024)(128)(4,1)S(1)}, s32[]{:S(2)}) async-start(s8[8388608]{0:T(1024)(128)(4,1)} %bitcast.53), calls=%async_computation.4 | async-start | bytes 8388608
  233.2 7.9 %copy-start.2 = (bf16[1,256,8192]{2,1,0:T(8,128)(2,1)S(1)}, bf16[1,256,8192]{2,1,0:T(8,128)(2,1)}, u32[]{:S(2)}) copy-start(bf16[1,256,8192]{2,1,0:T(8,128)(2,1)} %param.7) | copy-start | bytes 12582916
  233.2 7.9 %slice-start.1 = ((s8[8388608]{0:T(1024)(128)(4,1)}), s8[4194304]{0:T(1024)(128)(4,1)S(1)}, s32[]{:S(2)}) async-start(s8[8388608]{0:T(1024)(128)(4,1)} %bitcast.53), calls=%async_computation.5 | async-start | bytes 8388608
Sparse Core Ops, SparseCore 0:
  27.4 94.5 all-reduce.1
Sparse Core Ops, SparseCore 1:
  229.8 147.1 reduce-scatter.1
